TPU v7x, 256 devices: a whole 4x4x8 slice. The times are simulated.
256 devices in a mesh: dp: 32 (over z_lo, x, core), fsdp: 8 (over y, z_hi).
Axes of the slice: x: 4, y: 4, z: 8 (z_hi: 2, z_lo: 4; z = z_hi * 4 + z_lo), core: 2. Of those that a mesh axis runs over, the one named last changes fastest.
Arguments:
- latents: bfloat16 [128, 256, 4096], P('dp', 'fsdp'), may hold values from -6 to 6
- w_query: bfloat16 [4096, 2048], P('fsdp'), may hold values from -0.09375 to 0.09375
- w_out: bfloat16 [2048, 4096], P('fsdp'), may hold values from -0.125 to 0.125
- text_cache: bfloat16 [4, 128, 4096], replicated, may hold values from -128 to 128
- branch_counts: int32 [128], replicated, may hold values from 1 to 4, 192 in all
- branch_conds: int32 [128, 4], replicated, may hold values from 0 to 3
- guide_weights: int32 [4], replicated, may hold values from 1 to 8
- mod_scale: float32 [128, 4096], P('dp'), may hold values from -3 to 3
- mod_shift: float32 [128, 4096], P('dp'), may hold values from -6 to 6
Outputs:
- mixed: bfloat16 [128, 256, 4096], P('dp', 'fsdp')
Inputs may be any that keep to these rules, and one draw needn't show every extreme that they name: `branch_counts`: the counts sum to 192. `branch_conds`: entries past a latent's count are not used.
All inputs are finite; a program needn't handle non-finite values.
Results may differ from a plain program's by a relative error of at most 0.0086.
Values may be sent and summed in bfloat16 or wider, within the bound.
A program may use at most 128 MiB of HBM per device.

v0:
```python
import math

import jax
import jax.numpy as jnp
from jax import lax
from jax.sharding import PartitionSpec as P

HDIM = 128


def layer_norm(hidden):
    center = jnp.mean(hidden, axis=-1, keepdims=True)
    spread = jnp.mean((hidden - center) ** 2, axis=-1, keepdims=True)
    return (hidden - center) * lax.rsqrt(spread + 1e-06)


def attend(query_rows, table_row):
    total_rows = query_rows.shape[0]
    heads = query_rows.shape[1] // HDIM
    query_h = query_rows.reshape(total_rows, heads, HDIM)
    key_part = table_row[:, : heads * HDIM].reshape(-1, heads, HDIM)
    value_part = table_row[:, heads * HDIM :].reshape(-1, heads, HDIM)
    scores = jnp.einsum("rhd,thd->hrt", query_h, key_part, preferred_element_type=jnp.float32) * (
        1.0 / math.sqrt(HDIM)
    )
    peak = jnp.max(scores, axis=-1, keepdims=True)
    expd = jnp.exp(scores - peak)
    softmax_w = (expd / jnp.sum(expd, axis=-1, keepdims=True)).astype(jnp.bfloat16)
    result = jnp.einsum("hrt,thd->rhd", softmax_w, value_part, preferred_element_type=jnp.float32)
    return result.reshape(total_rows, heads * HDIM).astype(jnp.bfloat16)


def on_device(
    latents,
    w_query,
    w_out,
    text_cache,
    branch_counts,
    branch_conds,
    guide_weights,
    mod_scale,
    mod_shift,
):
    lat_dev, rows_here, width = latents.shape
    query_width = w_query.shape[1]
    guide_float = guide_weights.astype(jnp.float32)
    full_out = lax.all_gather(w_out, "fsdp", axis=0, tiled=True)
    flat_rows = latents.reshape(-1, width)
    product = jnp.dot(
        flat_rows,
        lax.all_gather(w_query, "fsdp", axis=0, tiled=True),
        preferred_element_type=jnp.float32,
    )
    queries = product.astype(jnp.bfloat16).reshape(lat_dev, rows_here, query_width)
    first_latent = lax.axis_index("dp") * lat_dev

    def per_latent(member, gathered):
        latent_id = first_latent + member
        count_here = lax.dynamic_index_in_dim(branch_counts, latent_id, 0, keepdims=False)
        cond_row = lax.dynamic_index_in_dim(branch_conds, latent_id, 0, keepdims=False)
        latent_x = lax.dynamic_index_in_dim(latents, member, 0, keepdims=False)
        latent_q = lax.dynamic_index_in_dim(queries, member, 0, keepdims=False)

        def per_slot(slot_idx, carry):
            numer, denom = carry
            table_row = lax.dynamic_index_in_dim(text_cache, cond_row[slot_idx], 0, keepdims=False)
            attended = attend(latent_q, table_row)
            hidden = latent_x.astype(jnp.float32) + jnp.dot(
                attended, full_out, preferred_element_type=jnp.float32
            )
            weight = guide_float[slot_idx]
            return (numer + weight * layer_norm(hidden), denom + weight)

        start = (jnp.zeros((rows_here, width), jnp.float32), jnp.zeros((), jnp.float32))
        numer, denom = lax.fori_loop(0, count_here, per_slot, start)
        combined = (numer / denom).astype(jnp.bfloat16)
        return lax.dynamic_update_index_in_dim(gathered, combined, member, 0)

    combined_all = lax.fori_loop(
        0, lat_dev, per_latent, jnp.zeros((lat_dev, rows_here, width), jnp.bfloat16)
    )
    modulated = (
        combined_all.astype(jnp.float32) * (1.0 + mod_scale[:, None, :]) + mod_shift[:, None, :]
    )
    return modulated.astype(jnp.bfloat16)


def solution(mesh):
    return jax.shard_map(
        on_device,
        mesh=mesh,
        in_specs=(
            P("dp", "fsdp", None),
            P("fsdp", None),
            P("fsdp", None),
            P(),
            P(),
            P(),
            P(),
            P("dp", None),
            P("dp", None),
        ),
        out_specs=P("dp", "fsdp", None),
        check_vma=False,
    )
```

profile of v0, /device:TPU:35, one launch (start us, length us, event | category | flops | bytes accessed | tf_op | source)
XLA Modules:
  0.0 808.2 jit_solution(18393367919865912705)
XLA Ops:
  8.1 6.4 copy.17
  15.9 301.5 %all-gather.3.cloned.1.call-done = bf16[4096,2048]{1,0:T(8,128)(2,1)} async-done(((bf16[512,2048]{1,0:T(8,128)(2,1)}), bf16[4096,2048]{1,0:T(8,128)(2,1)}) %all-gather.3.cloned.1.call-update) | async-done | bytes 16777232 | tf_op jit(solution)/shard_map/all_gather | solution.py:51
  317.4 8.1 %convolution_convert_fusion.1 = bf16[128,2048]{1,0:T(8,128)(2,1)S(1)} fusion(bf16[128,4096]{1,0:T(8,128)(2,1)S(1)} %bitcast.83, bf16[4096,2048]{1,0:T(8,128)(2,1)} %all-gather.3.cloned.1.call-done), kind=kOutput, calls=%fused_computation.26 | convolution fusion | flops 2147745792 | bytes 18350080 | tf_op jit(solution)/shard_map/dot_general | solution.py:49
  325.5 296.5 %all-gather.5.cloned.1.call-done = bf16[2048,4096]{1,0:T(8,128)(2,1)} async-done(((bf16[256,4096]{1,0:T(8,128)(2,1)}), bf16[2048,4096]{1,0:T(8,128)(2,1)}) %all-gather.5.cloned.1.call-update) | async-done | bytes 16777232 | tf_op jit(solution)/shard_map/all_gather | solution.py:47
  622.1 176.8 %while.42 = (s32[]{:T(128)}, bf16[4,32,4096]{2,1,0:T(8,128)(2,1)}, s32[]{:T(128)}, s32[128]{0:T(128)S(1)}, s32[128,4]{1,0:T(8,128)}, /*index=5*/bf16[4,32,2048]{...) while((s32[]{:T(128)}, bf16[4,32,4096]{2,1,0:T(8,128)(2,1)}, ...), condition=%wide.region_7.8_spmd, body=%wide.region_0.7_spmd.sunk | while | flops 572457792 | bytes 28187372 | solution.py:79
  624.0 55.2 %while.43 = (s32[]{:T(128)}, f32[32,4096]{1,0:T(8,128)S(1)}, f32[]{:T(128)}, s32[]{:T(128)}, f32[4]{0:T(128)S(1)}, /*index=5*/bf16[32,4096]{1,0:T(8,128)(2,1)S(1...) while((s32[]{:T(128)}, f32[32,4096]{1,0:T(8,128)S(1)}, ...), condition=%wide.region_6.6_spmd, body=%wide.region_1.5_spmd.sunk | while | flops 572195648 | bytes 26088812 | solution.py:75
  628.0 1.3 dynamic-slice_bitcast_fusion.8
  630.8 8.9 %fusion.48 = (f32[32]{0:T(128)S(1)}, f32[32,4096]{1,0:T(8,128)S(1)}) fusion(bf16[2048,4096]{1,0:T(8,128)(2,1)} %get-tuple-element.485, bf16[16,4,8,128]{3,2,1,0:T(8,128)(2,1)S(1)} %fusion.47, bf16[32,4096]{1,0:T(8,128)(2,1)S(1)} %get-tuple-element.481), kind=kOutput, calls=%fused_computation.31.clone.1 | convolution fusion | flops 537264128 | bytes 17694848 | tf_op jit(solution)/shard_map/while/body/eval_jaxpr/while/body/dot_general | solution.py:68
  646.2 1.3 dynamic-slice_bitcast_fusion.8
  648.9 8.9 %fusion.48 = (f32[32]{0:T(128)S(1)}, f32[32,4096]{1,0:T(8,128)S(1)}) fusion(bf16[2048,4096]{1,0:T(8,128)(2,1)} %get-tuple-element.485, bf16[16,4,8,128]{3,2,1,0:T(8,128)(2,1)S(1)} %fusion.47, bf16[32,4096]{1,0:T(8,128)(2,1)S(1)} %get-tuple-element.481), kind=kOutput, calls=%fused_computation.31.clone.1 | convolution fusion | flops 537264128 | bytes 17694848 | tf_op jit(solution)/shard_map/while/body/eval_jaxpr/while/body/dot_general | solution.py:68
  664.3 1.3 dynamic-slice_bitcast_fusion.8
  667.1 8.9 %fusion.48 = (f32[32]{0:T(128)S(1)}, f32[32,4096]{1,0:T(8,128)S(1)}) fusion(bf16[2048,4096]{1,0:T(8,128)(2,1)} %get-tuple-element.485, bf16[16,4,8,128]{3,2,1,0:T(8,128)(2,1)S(1)} %fusion.47, bf16[32,4096]{1,0:T(8,128)(2,1)S(1)} %get-tuple-element.481), kind=kOutput, calls=%fused_computation.31.clone.1 | convolution fusion | flops 537264128 | bytes 17694848 | tf_op jit(solution)/shard_map/while/body/eval_jaxpr/while/body/dot_general | solution.py:68
  681.8 37.0 %while.43 = (s32[]{:T(128)}, f32[32,4096]{1,0:T(8,128)S(1)}, f32[]{:T(128)}, s32[]{:T(128)}, f32[4]{0:T(128)S(1)}, /*index=5*/bf16[32,4096]{1,0:T(8,128)(2,1)S(1...) while((s32[]{:T(128)}, f32[32,4096]{1,0:T(8,128)S(1)}, ...), condition=%wide.region_6.6_spmd, body=%wide.region_1.5_spmd.sunk | while | flops 572195648 | bytes 26088812 | solution.py:75
  688.6 8.9 %fusion.48 = (f32[32]{0:T(128)S(1)}, f32[32,4096]{1,0:T(8,128)S(1)}) fusion(bf16[2048,4096]{1,0:T(8,128)(2,1)} %get-tuple-element.485, bf16[16,4,8,128]{3,2,1,0:T(8,128)(2,1)S(1)} %fusion.47, bf16[32,4096]{1,0:T(8,128)(2,1)S(1)} %get-tuple-element.481), kind=kOutput, calls=%fused_computation.31.clone.1 | convolution fusion | flops 537264128 | bytes 17694848 | tf_op jit(solution)/shard_map/while/body/eval_jaxpr/while/body/dot_general | solution.py:68
  706.8 8.9 %fusion.48 = (f32[32]{0:T(128)S(1)}, f32[32,4096]{1,0:T(8,128)S(1)}) fusion(bf16[2048,4096]{1,0:T(8,128)(2,1)} %get-tuple-element.485, bf16[16,4,8,128]{3,2,1,0:T(8,128)(2,1)S(1)} %fusion.47, bf16[32,4096]{1,0:T(8,128)(2,1)S(1)} %get-tuple-element.481), kind=kOutput, calls=%fused_computation.31.clone.1 | convolution fusion | flops 537264128 | bytes 17694848 | tf_op jit(solution)/shard_map/while/body/eval_jaxpr/while/body/dot_general | solution.py:68
  721.5 18.8 %while.43 = (s32[]{:T(128)}, f32[32,4096]{1,0:T(8,128)S(1)}, f32[]{:T(128)}, s32[]{:T(128)}, f32[4]{0:T(128)S(1)}, /*index=5*/bf16[32,4096]{1,0:T(8,128)(2,1)S(1...) while((s32[]{:T(128)}, f32[32,4096]{1,0:T(8,128)S(1)}, ...), condition=%wide.region_6.6_spmd, body=%wide.region_1.5_spmd.sunk | while | flops 572195648 | bytes 26088812 | solution.py:75
  728.3 8.9 %fusion.48 = (f32[32]{0:T(128)S(1)}, f32[32,4096]{1,0:T(8,128)S(1)}) fusion(bf16[2048,4096]{1,0:T(8,128)(2,1)} %get-tuple-element.485, bf16[16,4,8,128]{3,2,1,0:T(8,128)(2,1)S(1)} %fusion.47, bf16[32,4096]{1,0:T(8,128)(2,1)S(1)} %get-tuple-element.481), kind=kOutput, calls=%fused_computation.31.clone.1 | convolution fusion | flops 537264128 | bytes 17694848 | tf_op jit(solution)/shard_map/while/body/eval_jaxpr/while/body/dot_general | solution.py:68
  742.9 55.2 %while.43 = (s32[]{:T(128)}, f32[32,4096]{1,0:T(8,128)S(1)}, f32[]{:T(128)}, s32[]{:T(128)}, f32[4]{0:T(128)S(1)}, /*index=5*/bf16[32,4096]{1,0:T(8,128)(2,1)S(1...) while((s32[]{:T(128)}, f32[32,4096]{1,0:T(8,128)S(1)}, ...), condition=%wide.region_6.6_spmd, body=%wide.region_1.5_spmd.sunk | while | flops 572195648 | bytes 26088812 | solution.py:75
  746.9 1.3 dynamic-slice_bitcast_fusion.8
  749.7 8.9 %fusion.48 = (f32[32]{0:T(128)S(1)}, f32[32,4096]{1,0:T(8,128)S(1)}) fusion(bf16[2048,4096]{1,0:T(8,128)(2,1)} %get-tuple-element.485, bf16[16,4,8,128]{3,2,1,0:T(8,128)(2,1)S(1)} %fusion.47, bf16[32,4096]{1,0:T(8,128)(2,1)S(1)} %get-tuple-element.481), kind=kOutput, calls=%fused_computation.31.clone.1 | convolution fusion | flops 537264128 | bytes 17694848 | tf_op jit(solution)/shard_map/while/body/eval_jaxpr/while/body/dot_general | solution.py:68
  767.9 8.9 %fusion.48 = (f32[32]{0:T(128)S(1)}, f32[32,4096]{1,0:T(8,128)S(1)}) fusion(bf16[2048,4096]{1,0:T(8,128)(2,1)} %get-tuple-element.485, bf16[16,4,8,128]{3,2,1,0:T(8,128)(2,1)S(1)} %fusion.47, bf16[32,4096]{1,0:T(8,128)(2,1)S(1)} %get-tuple-element.481), kind=kOutput, calls=%fused_computation.31.clone.1 | convolution fusion | flops 537264128 | bytes 17694848 | tf_op jit(solution)/shard_map/while/body/eval_jaxpr/while/body/dot_general | solution.py:68
  783.3 1.3 dynamic-slice_bitcast_fusion.8
  786.1 8.9 %fusion.48 = (f32[32]{0:T(128)S(1)}, f32[32,4096]{1,0:T(8,128)S(1)}) fusion(bf16[2048,4096]{1,0:T(8,128)(2,1)} %get-tuple-element.485, bf16[16,4,8,128]{3,2,1,0:T(8,128)(2,1)S(1)} %fusion.47, bf16[32,4096]{1,0:T(8,128)(2,1)S(1)} %get-tuple-element.481), kind=kOutput, calls=%fused_computation.31.clone.1 | convolution fusion | flops 537264128 | bytes 17694848 | tf_op jit(solution)/shard_map/while/body/eval_jaxpr/while/body/dot_general | solution.py:68
  798.9 2.5 add_convert_fusion
  (140 shorter events, 59.8 us)
Async XLA Ops:
  6.5 310.9 %all-gather.3.cloned.1.call-start = ((), (), s32[]{:S(2)}) async-start(), calls=%async_computation | async-start | bytes 18874368 | tf_op jit(solution)/shard_map/all_gather | solution.py:51
  7.3 614.8 %all-gather.5.cloned.1.call-start = ((), (), s32[]{:S(2)}) async-start(), calls=%async_computation.1 | async-start | bytes 18874368 | tf_op jit(solution)/shard_map/all_gather | solution.py:47
  8.0 6.5 copy-start.4
  8.0 7.2 copy-start.5
  8.0 7.2 copy-start.3
  8.1 309.4 %copy-start = (bf16[4,32,4096]{2,1,0:T(8,128)(2,1)S(1)}, bf16[4,32,4096]{2,1,0:T(8,128)(2,1)}, u32[]{:S(2)}) copy-start(bf16[4,32,4096]{2,1,0:T(8,128)(2,1)} %param.13) | copy-start | bytes 3145732
  317.4 304.7 %copy-start.6 = (s32[128]{0:T(128)S(1)}, s32[128]{0:T(128)}, u32[]{:S(2)}) copy-start(s32[128]{0:T(128)} %param.17) | copy-start | bytes 1540
  622.1 176.8 %copy-start.1 = (f32[4,4096]{1,0:T(4,128)S(1)}, f32[4,4096]{1,0:T(4,128)}, u32[]{:S(2)}) copy-start(f32[4,4096]{1,0:T(4,128)} %broadcast_add_fusion) | copy-start | bytes 196612
  622.1 176.8 %copy-start.2 = (f32[4,4096]{1,0:T(4,128)S(1)}, f32[4,4096]{1,0:T(4,128)}, u32[]{:S(2)}) copy-start(f32[4,4096]{1,0:T(4,128)} %param.21) | copy-start | bytes 196612
Sparse Core Ops, SparseCore 0:
  10.0 307.3 all-gather.2
  320.0 301.9 all-gather.4
where the time goes:
time: 810 us; the launch traced here: 808 us
  waiting for transfers between devices  599 us (74%)
  matrix products  98.2 us (12%)
  local copies, waits for them, and re-layouts  44.5 us (5%)
  loops' own time  33.7 us (4%)
  other arithmetic  18.8 us (2%)
  between operations  13.5 us (2%)
    all_gather x1, waiting for transfers between devices, on_device(): lax.all_gather(w_query, 'fsdp', axis=0, tiled=True)  301 us
    all_gather x1, waiting for transfers between devices, on_device(): full_out = lax.all_gather(w_out, 'fsdp', axis=0, tiled=True)  297 us
    dot_general x9, matrix products, per_slot(): jnp.dot(attended, full_out, preferred_element_type=jnp.float32)  79.7 us
    another operation x4, loops' own time, per_latent(): numer, denom = lax.fori_loop(0, count_here, per_slot, start)  33.6 us
  transfers between devices with their start and end apart: 2, of which 2 were waited for; matrix products, arithmetic and copies ran while one was open for 2% of the time, Pallas kernels for 0%

commit v1 on v0

v1 whole, which is shorter than its diff:
```python
import functools
import math

import jax
import jax.numpy as jnp
from jax import lax
from jax.experimental import pallas as pl
from jax.experimental.pallas import tpu as pltpu
from jax.sharding import PartitionSpec as P

HDIM = 128
MESH = pl.DeviceIdType.MESH
LAG = 3
KGROUPS = 4
RELAY_LAG = 2
PREFS = {
    "x": (-1.1011020595399832, -1.9026346360323592, 2.1056340006474246),
    "y": (2.9389532323178447, -2.1789154677931455, 2.885831829951437),
    "z": (-2.8608332355771946, 2.8185845334998927, 1.2925265631373692),
}
CHAIN_PREF = 2.5997267012272784
QUERY_PREF = 5.0
GROUP_PREF = 1.0


def moved(link, place, piece):
    dy, h, k, r = piece
    if link == 0:
        return place, (dy, h, k, (r + 1) % 4)
    if link == 1:
        return place, ((dy + 1) % 4, h, k, r)
    if place < 3:
        return place + 1, piece
    return 0, (dy, 1 - h, k, r)


def make_rounds():
    pieces = [
        (dy, h, k, r) for dy in range(4) for h in range(2) for k in range(KGROUPS) for r in range(4)
    ]
    ready = [{p: 0 if p[:2] == (0, 0) else 1 << 30 for p in pieces} for _ in range(4)]
    taken = [{p: p[:2] == (0, 0) for p in pieces} for _ in range(4)]
    worth = {}
    for link, name in enumerate("xyz"):
        half, depth, column = PREFS[name]
        for p in pieces:
            worth[link, p] = (
                (QUERY_PREF if p[2] < KGROUPS // 2 else 0.0)
                - GROUP_PREF * p[2]
                + half * p[1]
                + depth * p[0]
                + column * p[3]
            )
    left = 4 * (len(pieces) - KGROUPS * 4)
    rounds = []
    while left:
        now = len(rounds)
        row = [[None] * 4 for _ in range(3)]
        for link in (2, 1, 0):
            for place in range(4):
                best, best_worth = None, -1e18
                for p in pieces:
                    if ready[place][p] <= now:
                        to, there = moved(link, place, p)
                        if not taken[to][there]:
                            w = worth[link, there]
                            if link == 2:
                                w += CHAIN_PREF * there[1] * (3 - to)
                            if w > best_worth:
                                best, best_worth = (p, to, there), w
                if best is not None:
                    p, to, there = best
                    taken[to][there] = True
                    ready[to][there] = now + LAG
                    left -= 1
                    row[link][place] = p
        rounds.append(row)
    return rounds, ready


def arrivals_of(rounds):
    result = []
    for row in rounds:
        got = [[None] * 4 for _ in range(3)]
        for link in range(3):
            for place in range(4):
                if row[link][place] is not None:
                    to, there = moved(link, place, row[link][place])
                    got[link][to] = there
        result.append(got)
    return result


def shard_ready(ready, groups):
    result = {}
    for dy in range(4):
        for h in range(2):
            last = 0
            if (dy, h) != (0, 0):
                for place in range(4):
                    for k in groups:
                        for r in range(4):
                            mine = ready[place][dy, h, k, r]
                            other = ready[3 - place][(4 - dy) % 4, h, k, r] + RELAY_LAG
                            last = max(last, mine, other)
            result[dy, h] = last
    return result


def kernel(
    n_dp,
    lat_ref,
    wq_ref,
    wo_ref,
    text_ref,
    counts_ref,
    conds_ref,
    guide_ref,
    scale_ref,
    shift_ref,
    out_ref,
    wq,
    wo,
    x_buf,
    text,
    q_acc,
    att,
    acc,
    send_sem,
    recv_sem,
    relay_sem,
    sib_sem,
    local_sem,
):
    rounds, ready = make_rounds()
    arrivals = arrivals_of(rounds)
    n_rounds = len(rounds)
    dp, fs = lax.axis_index("dp"), lax.axis_index("fsdp")
    core, x_at, z_lo = dp % 2, (dp // 2) % 4, dp // 8
    y_at, z_hi = fs // 2, fs % 2
    sign = 1 - 2 * core
    column = (4 + sign * x_at) % 4
    place = z_lo + core * (3 - 2 * z_lo)
    z_next = (z_hi * 4 + z_lo + 8 + sign) % 8
    z_prev = (z_hi * 4 + z_lo + 8 - sign) % 8
    targets = (
        (z_lo * 8 + ((x_at + 4 + sign) % 4) * 2 + core, fs),
        (dp, ((y_at + 4 + sign) % 4) * 2 + z_hi),
        ((z_next % 4) * 8 + x_at * 2 + core, y_at * 2 + z_next // 4),
    )
    sources = (
        (z_lo * 8 + ((x_at + 4 - sign) % 4) * 2 + core, fs),
        (dp, ((y_at + 4 - sign) % 4) * 2 + z_hi),
        ((z_prev % 4) * 8 + x_at * 2 + core, y_at * 2 + z_prev // 4),
    )
    sibling = (dp + sign, fs)

    fetches = [
        pltpu.make_async_copy(wq_ref, wq.at[fs], local_sem.at[0]),
        pltpu.make_async_copy(wo_ref, wo.at[fs], local_sem.at[1]),
        pltpu.make_async_copy(lat_ref, x_buf, local_sem.at[2]),
        pltpu.make_async_copy(text_ref, text, local_sem.at[3]),
    ]
    for fetch in fetches:
        fetch.start()
    barrier = pltpu.get_barrier_semaphore()
    for other in sources + (sibling,):
        pl.semaphore_signal(barrier, inc=1, device_id=other, device_id_type=MESH)
    pl.semaphore_wait(barrier, 4)
    fetches[0].wait()
    fetches[1].wait()

    def shard_of(dy, h):
        return ((y_at + 4 - sign * dy) % 4) * 2 + (z_hi + h) % 2

    def pick(options, field):
        values = {p: options[p][field] for p in options}
        if len(set(values.values())) == 1:
            return next(iter(values.values()))
        result, items = None, list(values.items())
        result = items[-1][1]
        for p, v in items[:-1]:
            result = jnp.where(place == p, v, result)
        return result

    def slot(options, weight):
        shard = shard_of(pick(options, 0), pick(options, 1))
        number = (pick(options, 2) % 2) * 4 + (column + 4 - pick(options, 3)) % 4
        if weight == 0:
            return wq.at[shard, pl.ds(pl.multiple_of(core * 256 + number * 32, 32), 32)], shard
        return wo.at[shard, pl.ds(pl.multiple_of(core * 128 + number * 16, 16), 16)], shard

    def for_places(row, action):
        for weight in range(2):
            options = {
                p: row[p] for p in range(4) if row[p] is not None and row[p][2] // 2 == weight
            }
            if not options:
                continue
            if len(options) == 4:
                action(options, weight)
            else:
                here = functools.reduce(jnp.logical_or, [place == p for p in options])
                pl.when(here)(functools.partial(action, options, weight))

    def link_copy(link, step, options, weight):
        ref, _ = slot(options, weight)
        return pltpu.make_async_remote_copy(
            src_ref=ref,
            dst_ref=ref,
            send_sem=send_sem.at[link * n_rounds + step],
            recv_sem=recv_sem.at[link * n_rounds + step],
            device_id=targets[link],
            device_id_type=MESH,
        )

    def relay_copy(link, step, options, weight):
        ref, shard = slot(options, weight)
        return pltpu.make_async_remote_copy(
            src_ref=ref,
            dst_ref=ref,
            send_sem=relay_sem.at[link * n_rounds + step],
            recv_sem=sib_sem.at[weight * 8 + shard],
            device_id=sibling,
            device_id_type=MESH,
        )

    def wait_sibling(weight, shard):
        if weight == 0:
            ref = wq.at[shard, pl.ds(pl.multiple_of((1 - core) * 256, 256), 256)]
        else:
            ref = wo.at[shard, pl.ds(pl.multiple_of((1 - core) * 128, 128), 128)]
        pltpu.make_async_copy(ref, ref, sib_sem.at[weight * 8 + shard]).wait()

    def query_task(index, dy, h):
        shard = shard_of(dy, h)
        if (dy, h) != (0, 0):
            wait_sibling(0, shard)
        rows = x_buf[:, pl.ds(pl.multiple_of(shard * 512, 512), 512)]

        @pl.loop(0, 4)
        def _(tile):
            at = pl.ds(pl.multiple_of(tile * 512, 512), 512)
            part = jnp.dot(rows, wq[shard, :, at], preferred_element_type=jnp.float32)
            if index == 0:
                q_acc[:, at] = part
            else:
                q_acc[:, at] += part

    def attend_task(first, count):
        @pl.loop(first, first + count)
        def _(head):
            at = pl.ds(pl.multiple_of(head * HDIM, HDIM), HDIM)
            value_at = pl.ds(pl.multiple_of(2048 + head * HDIM, HDIM), HDIM)
            queries = q_acc[:, at].astype(jnp.bfloat16)
            for cond in range(4):
                scores = lax.dot_general(
                    queries,
                    text[cond, :, at],
                    (((1,), (1,)), ((), ())),
                    preferred_element_type=jnp.float32,
                ) * (1.0 / math.sqrt(HDIM))
                expd = jnp.exp(scores - jnp.max(scores, axis=-1, keepdims=True))
                probs = (expd / jnp.sum(expd, axis=-1, keepdims=True)).astype(jnp.bfloat16)
                result = jnp.dot(
                    probs, text[cond, :, value_at], preferred_element_type=jnp.float32
                )
                att[pl.ds(cond * 128, 128), at] = result.astype(jnp.bfloat16)

    def out_task(index, dy, h):
        shard = shard_of(dy, h)
        if (dy, h) != (0, 0):
            wait_sibling(1, shard)
        rows_at = pl.ds(pl.multiple_of(shard * 256, 256), 256)

        @pl.loop(0, 8)
        def _(tile):
            at = pl.ds(pl.multiple_of(tile * 512, 512), 512)
            part = jnp.dot(att[:, rows_at], wo[shard, :, at], preferred_element_type=jnp.float32)
            if index == 0:
                base = x_buf[:, at].astype(jnp.float32)
                acc[:, at] = part + jnp.concatenate([base] * 4, axis=0)
            else:
                acc[:, at] += part

    query_ready = shard_ready(ready, range(KGROUPS // 2))
    out_ready = shard_ready(ready, range(KGROUPS // 2, KGROUPS))
    tasks = []
    for i, s in enumerate(sorted(query_ready, key=lambda s: (query_ready[s], s))):
        tasks.append((query_ready[s], functools.partial(query_task, i, *s)))
    for first in range(0, 16, 2):
        tasks.append((0, functools.partial(attend_task, first, 2)))
    for i, s in enumerate(sorted(out_ready, key=lambda s: (out_ready[s], s))):
        tasks.append((out_ready[s], functools.partial(out_task, i, *s)))

    fetched = False
    for step in range(n_rounds + LAG):
        came = step - LAG
        if came >= 0:
            for link in range(3):
                for_places(
                    arrivals[came][link],
                    lambda options, weight, link=link: link_copy(
                        link, came, options, weight
                    ).wait_recv(),
                )
        if step < n_rounds:
            for link in range(3):
                for_places(
                    rounds[step][link],
                    lambda options, weight, link=link: link_copy(
                        link, step, options, weight
                    ).start(),
                )
        if came >= 0:
            for link in range(3):
                for_places(
                    arrivals[came][link],
                    lambda options, weight, link=link: relay_copy(
                        link, came, options, weight
                    ).start(),
                )
        if step >= 1:
            if not fetched:
                fetches[2].wait()
                fetches[3].wait()
                fetched = True
            if tasks and tasks[0][0] <= step:
                tasks.pop(0)[1]()
    for _, task in tasks:
        task()

    @pl.loop(0, 4)
    def _(member):
        latent = dp * 4 + member
        count = counts_ref[latent]
        total = jnp.int32(0)
        weights = [jnp.int32(0)] * 4
        for s in range(4):
            weight = jnp.where(s < count, guide_ref[s], 0)
            total = total + weight
            cond = conds_ref[s, latent]
            weights = [w + jnp.where(cond == c, weight, 0) for c, w in enumerate(weights)]
        total = total.astype(jnp.float32)
        weights = [w.astype(jnp.float32) for w in weights]
        scale = 1.0 + scale_ref[pl.ds(member, 1), :]
        shift = shift_ref[pl.ds(member, 1), :]

        @pl.loop(0, 2)
        def _(block):
            start = pl.multiple_of(member * 32 + block * 16, 16)
            numer = jnp.zeros((16, 4096), jnp.float32)
            for cond in range(4):
                hidden = acc[pl.ds(pl.multiple_of(cond * 128 + start, 16), 16), :]
                center = jnp.mean(hidden, axis=-1, keepdims=True)
                moved_h = hidden - center
                spread = jnp.mean(moved_h * moved_h, axis=-1, keepdims=True)
                numer += moved_h * (weights[cond] * lax.rsqrt(spread + 1e-06))
            combined = (numer / total).astype(jnp.bfloat16).astype(jnp.float32)
            out_ref[pl.ds(start, 16), :] = (combined * scale + shift).astype(jnp.bfloat16)

    for step in range(n_rounds):
        for link in range(3):
            for_places(
                rounds[step][link],
                lambda options, weight, link=link: link_copy(
                    link, step, options, weight
                ).wait_send(),
            )
            for_places(
                arrivals[step][link],
                lambda options, weight, link=link: relay_copy(
                    link, step, options, weight
                ).wait_send(),
            )


def on_device(
    n_dp,
    latents,
    w_query,
    w_out,
    text_cache,
    branch_counts,
    branch_conds,
    guide_weights,
    mod_scale,
    mod_shift,
):
    members, rows_here, width = latents.shape
    rows = members * rows_here
    n_rounds = len(make_rounds()[0])
    anywhere = pl.BlockSpec(memory_space=pl.ANY)
    in_vmem = pl.BlockSpec(memory_space=pltpu.VMEM)
    in_smem = pl.BlockSpec(memory_space=pltpu.SMEM)
    mixed = pl.pallas_call(
        functools.partial(kernel, n_dp),
        out_shape=jax.ShapeDtypeStruct((rows, width), jnp.bfloat16),
        in_specs=[anywhere] * 4 + [in_smem] * 3 + [in_vmem] * 2,
        out_specs=in_vmem,
        scratch_shapes=[
            pltpu.VMEM((8, 512, 2048), jnp.bfloat16),
            pltpu.VMEM((8, 256, 4096), jnp.bfloat16),
            pltpu.VMEM((rows, width), jnp.bfloat16),
            pltpu.VMEM(text_cache.shape, jnp.bfloat16),
            pltpu.VMEM((rows, 2048), jnp.float32),
            pltpu.VMEM((4 * rows, 2048), jnp.bfloat16),
            pltpu.VMEM((4 * rows, width), jnp.float32),
            pltpu.SemaphoreType.DMA((3 * n_rounds,)),
            pltpu.SemaphoreType.DMA((3 * n_rounds,)),
            pltpu.SemaphoreType.DMA((3 * n_rounds,)),
            pltpu.SemaphoreType.DMA((16,)),
            pltpu.SemaphoreType.DMA((4,)),
        ],
        compiler_params=pltpu.CompilerParams(
            collective_id=0, has_side_effects=True, vmem_limit_bytes=58 * 2**20
        ),
        name="gather_and_attend",
    )(
        latents.reshape(rows, width),
        w_query,
        w_out,
        text_cache,
        branch_counts,
        branch_conds.T,
        guide_weights,
        mod_scale,
        mod_shift,
    )
    return mixed.reshape(members, rows_here, width)


def solution(mesh):
    return jax.shard_map(
        functools.partial(on_device, mesh.shape["dp"]),
        mesh=mesh,
        in_specs=(
            P("dp", "fsdp", None),
            P("fsdp", None),
            P("fsdp", None),
            P(),
            P(),
            P(),
            P(),
            P("dp", None),
            P("dp", None),
        ),
        out_specs=P("dp", "fsdp", None),
        check_vma=False,
    )
```

time: 810 us -> 111 us (0.14)
  the two profiles are of different devices: /device:TPU:35 before, /device:TPU:1 now
where the time goes in v1:
time: 111 us; the launch traced here: 110 us
  Pallas kernels  108 us (97%)
  local copies, waits for them, and re-layouts  2.29 us (2%)
    pallas_call x1, Pallas kernels, on_device(): pl.pallas_call(functools.partial(kernel, n_dp), out_shape=jax.ShapeDtypeS...  108 us
    unnamed x1, local copies, waits for them, and re-layouts  2.29 us

profile of v1, /device:TPU:1, one launch (start us, length us, event | category | flops | bytes accessed | tf_op | source)
XLA Modules:
  0.0 110.2 jit_solution(18291431444790508472)
XLA Ops:
  0.0 107.9 %gather_and_attend.1 = bf16[128,4096]{1,0:T(8,128)(2,1)} custom-call(bf16[128,4096]{1,0:T(8,128)(2,1)} %bitcast.4, bf16[512,2048]{1,0:T(8,128)(2,1)} %wq_ref.1, bf16[256,4096]{1,0:T(8,128)(2,1)} %wo_ref.1, bf16[4,128,4096]{2,1,0:T(8,128)(2,1)} %text_ref.1, s32[128]{0:T(128)} %counts_ref.1, s32[4,128]{1,0:T(4,128)} %bitcast.5, s32[4]{0:T(128)} %guide_ref.1, ...), custom_call_target="tpu_custom_call" | custom-call | tf_op jit(solution)/shard_map/gather_and_attend/pallas_call | solution.py:396
  107.9 2.3 %copy.11 = bf16[4,32,4096]{2,1,0:T(8,128)(2,1)} copy(bf16[4,32,4096]{2,1,0:T(8,128)(2,1)} %bitcast.3) | data formatting | bytes 2097152

commit v2 on v1

v2 whole, which is shorter than its diff:
```python
import functools
import math

import jax
import jax.numpy as jnp
from jax import lax
from jax.experimental import pallas as pl
from jax.experimental.pallas import tpu as pltpu
from jax.sharding import PartitionSpec as P

HDIM = 128
MESH = pl.DeviceIdType.MESH
LAG = 3
KGROUPS = 4
RELAY_LAG = 2
PREFS = {
    "x": (1.5859338734408208, 2.214087352289587, 2.9301547809913906),
    "y": (1.1536104177094657, 1.5604518340377975, 1.8994994812664077),
    "z": (-2.091808917993905, 1.831880295654794, -1.8133725211069505),
}
CHAIN_PREF = 2.3398409033170617
GROUP_PREF = 0.5
LINK_ORDER = (0, 2, 1)
ROUND_US = 1.2
QUERY_US, ATTEND_US, OUT_US = 0.27, 0.72, 0.72
LAST_SHARDS = 3


def moved(link, place, piece):
    dy, h, k, r = piece
    if link == 0:
        return place, (dy, h, k, (r + 1) % 4)
    if link == 1:
        return place, ((dy + 1) % 4, h, k, r)
    if place < 3:
        return place + 1, piece
    return 0, (dy, 1 - h, k, r)


def make_rounds():
    pieces = [
        (dy, h, k, r) for dy in range(4) for h in range(2) for k in range(KGROUPS) for r in range(4)
    ]
    ready = [{p: 0 if p[:2] == (0, 0) else 1 << 30 for p in pieces} for _ in range(4)]
    taken = [{p: p[:2] == (0, 0) for p in pieces} for _ in range(4)]
    worth = {}
    for link, name in enumerate("xyz"):
        half, depth, column = PREFS[name]
        for p in pieces:
            worth[link, p] = (
                -GROUP_PREF * p[2]
                + half * p[1]
                + depth * p[0]
                + column * p[3]
            )
    left = 4 * (len(pieces) - KGROUPS * 4)
    rounds = []
    while left:
        now = len(rounds)
        row = [[None] * 4 for _ in range(3)]
        for link in LINK_ORDER:
            for place in range(4):
                best, best_worth = None, -1e18
                for p in pieces:
                    if ready[place][p] <= now:
                        to, there = moved(link, place, p)
                        if not taken[to][there]:
                            w = worth[link, there]
                            if link == 2:
                                w += CHAIN_PREF * there[1] * (3 - to)
                            if w > best_worth:
                                best, best_worth = (p, to, there), w
                if best is not None:
                    p, to, there = best
                    taken[to][there] = True
                    ready[to][there] = now + LAG
                    left -= 1
                    row[link][place] = p
        rounds.append(row)
    return rounds, ready


def arrivals_of(rounds):
    result = []
    for row in rounds:
        got = [[None] * 4 for _ in range(3)]
        for link in range(3):
            for place in range(4):
                if row[link][place] is not None:
                    to, there = moved(link, place, row[link][place])
                    got[link][to] = there
        result.append(got)
    return result


def group_rounds(ready):
    mine, both = {}, {}
    for dy in range(4):
        for h in range(2):
            for k in range(KGROUPS):
                mine[dy, h, k] = max(ready[place][dy, h, k, r] for place in range(4) for r in range(4))
    for dy, h, k in mine:
        both[dy, h, k] = max(mine[dy, h, k], mine[(4 - dy) % 4, h, k] + RELAY_LAG)
        if (dy, h) == (0, 0):
            both[dy, h, k] = 0
    return mine, both


def kernel(
    n_dp,
    lat_ref,
    wq_ref,
    wo_ref,
    text_ref,
    counts_ref,
    conds_ref,
    guide_ref,
    scale_ref,
    shift_ref,
    out_ref,
    wq,
    wo,
    x_buf,
    text,
    q_acc,
    att,
    acc,
    send_sem,
    recv_sem,
    sib_sem,
    local_sem,
):
    rounds, ready = make_rounds()
    arrivals = arrivals_of(rounds)
    n_rounds = len(rounds)
    dp, fs = lax.axis_index("dp"), lax.axis_index("fsdp")
    core, x_at, z_lo = dp % 2, (dp // 2) % 4, dp // 8
    y_at, z_hi = fs // 2, fs % 2
    sign = 1 - 2 * core
    column = (4 + sign * x_at) % 4
    place = z_lo + core * (3 - 2 * z_lo)
    z_next = (z_hi * 4 + z_lo + 8 + sign) % 8
    z_prev = (z_hi * 4 + z_lo + 8 - sign) % 8
    targets = (
        (z_lo * 8 + ((x_at + 4 + sign) % 4) * 2 + core, fs),
        (dp, ((y_at + 4 + sign) % 4) * 2 + z_hi),
        ((z_next % 4) * 8 + x_at * 2 + core, y_at * 2 + z_next // 4),
    )
    sources = (
        (z_lo * 8 + ((x_at + 4 - sign) % 4) * 2 + core, fs),
        (dp, ((y_at + 4 - sign) % 4) * 2 + z_hi),
        ((z_prev % 4) * 8 + x_at * 2 + core, y_at * 2 + z_prev // 4),
    )
    sibling = (dp + sign, fs)

    fetches = [
        pltpu.make_async_copy(wq_ref, wq.at[fs], local_sem.at[0]),
        pltpu.make_async_copy(wo_ref, wo.at[fs], local_sem.at[1]),
        pltpu.make_async_copy(lat_ref, x_buf, local_sem.at[2]),
        pltpu.make_async_copy(text_ref, text, local_sem.at[3]),
    ]
    for fetch in fetches:
        fetch.start()
    barrier = pltpu.get_barrier_semaphore()
    for other in sources + (sibling,):
        pl.semaphore_signal(barrier, inc=1, device_id=other, device_id_type=MESH)
    pl.semaphore_wait(barrier, 4)
    fetches[0].wait()
    fetches[1].wait()

    shards = {
        (dy, h): ((y_at + 4 - sign * dy) % 4) * 2 + (z_hi + h) % 2 for dy in range(4) for h in range(2)
    }
    columns = [(column + 4 - r) % 4 for r in range(4)]
    row_at = (
        [core * 256 + c * 64 for c in columns],
        [core * 128 + c * 32 for c in columns],
    )

    def pick(options, of):
        keyed = {}
        for p, piece in options.items():
            key, value = of(piece)
            keyed.setdefault(key, (value, []))[1].append(p)
        groups = list(keyed.values())
        result = groups[-1][0]
        for value, places in groups[:-1]:
            here = functools.reduce(jnp.logical_or, [place == p for p in places])
            result = jnp.where(here, value, result)
        return result

    def slot(options, weight):
        shard = pick(options, lambda p: (p[:2], shards[p[:2]]))
        row = pick(options, lambda p: (p[3], row_at[weight][p[3]]))
        half = pick(options, lambda p: (p[2] % 2, p[2] % 2))
        if weight == 0:
            return wq.at[
                shard,
                pl.ds(pl.multiple_of(row, 64), 64),
                pl.ds(pl.multiple_of(half * 1024, 1024), 1024),
            ]
        return wo.at[
            shard,
            pl.ds(pl.multiple_of(row, 32), 32),
            pl.ds(pl.multiple_of(half * 2048, 2048), 2048),
        ]

    def for_places(row, action):
        for weight in range(2):
            options = {
                p: row[p] for p in range(4) if row[p] is not None and row[p][2] // 2 == weight
            }
            if not options:
                continue
            if len(options) == 4:
                action(options, weight)
            else:
                here = functools.reduce(jnp.logical_or, [place == p for p in options])
                pl.when(here)(functools.partial(action, options, weight))

    def link_copy(link, step, options, weight):
        ref = slot(options, weight)
        return pltpu.make_async_remote_copy(
            src_ref=ref,
            dst_ref=ref,
            send_sem=send_sem.at[link],
            recv_sem=recv_sem.at[link * n_rounds + step],
            device_id=targets[link],
            device_id_type=MESH,
        )

    def half_group(dy, h, k, of_core):
        shard = shards[dy, h]
        if k < 2:
            rows = pl.ds(pl.multiple_of(of_core * 256, 256), 256)
            return wq.at[shard, rows, pl.ds(k * 1024, 1024)], sib_sem.at[k * 8 + shard]
        rows = pl.ds(pl.multiple_of(of_core * 128, 128), 128)
        return wo.at[shard, rows, pl.ds((k - 2) * 2048, 2048)], sib_sem.at[k * 8 + shard]

    def relay(dy, h, k):
        ref, sem = half_group(dy, h, k, core)
        pltpu.make_async_remote_copy(
            src_ref=ref,
            dst_ref=ref,
            send_sem=send_sem.at[3],
            recv_sem=sem,
            device_id=sibling,
            device_id_type=MESH,
        ).start()

    def wait_sibling(dy, h, k):
        if (dy, h) != (0, 0):
            ref, sem = half_group(dy, h, k, 1 - core)
            pltpu.make_async_copy(ref, ref, sem).wait()

    def wait_sent(sem, ref):
        pltpu.make_async_copy(ref, ref, sem).wait()

    mine, both = group_rounds(ready)
    order = sorted(shards, key=lambda s: (both[s + (3,)], s))
    places_of = []
    for shard in range(8):
        back = (sign * (y_at - shard // 2) + 4) % 4
        key = back * 2 + (z_hi + shard) % 2
        at = jnp.int32(0)
        for i, (dy, h) in enumerate(order):
            at = jnp.where(key == dy * 2 + h, i, at)
        places_of.append(at * 256)

    def query_task(first, dy, h, k):
        wait_sibling(dy, h, k)
        shard = shards[dy, h]
        at = pl.ds(k * 1024, 1024)
        part = jnp.dot(
            x_buf[:, pl.ds(pl.multiple_of(shard * 512, 512), 512)],
            wq[shard, :, at],
            preferred_element_type=jnp.float32,
        )
        if first:
            q_acc[:, at] = part
        else:
            q_acc[:, at] += part

    def attend_task(shard):
        scored = []
        for p in range(2):
            head = shard * 2 + p
            queries = q_acc[:, head * HDIM : (head + 1) * HDIM].astype(jnp.bfloat16)
            for cond in range(4):
                scores = lax.dot_general(
                    queries,
                    text[cond, :, head * HDIM : (head + 1) * HDIM],
                    (((1,), (1,)), ((), ())),
                    preferred_element_type=jnp.float32,
                )
                scored.append((p, cond, scores))
        weighed = []
        for p, cond, scores in scored:
            peak = jnp.max(scores, axis=-1, keepdims=True)
            expd = jnp.exp2((scores - peak) * (math.log2(math.e) / math.sqrt(HDIM)))
            probs = (expd * (1.0 / jnp.sum(expd, axis=-1, keepdims=True))).astype(jnp.bfloat16)
            weighed.append((p, cond, probs))
        for p, cond, probs in weighed:
            value_at = 2048 + (shard * 2 + p) * HDIM
            result = jnp.dot(
                probs, text[cond, :, value_at : value_at + HDIM], preferred_element_type=jnp.float32
            )
            at = pl.ds(pl.multiple_of(places_of[shard] + p * HDIM, HDIM), HDIM)
            att[pl.ds(cond * 128, 128), at] = result.astype(jnp.bfloat16)

    def out_task(low, high, start, width, k):
        if start == (k - 2) * 2048:
            for dy, h in order[low:high]:
                wait_sibling(dy, h, k)
        at = pl.ds(start, width)
        part = jnp.dot(
            att[:, low * 256 : high * 256],
            jnp.concatenate([wo[shards[s], :, at] for s in order[low:high]], axis=0),
            preferred_element_type=jnp.float32,
        )
        if low == 0:
            base = x_buf[:, at].astype(jnp.float32)
            acc[:, at] = part + jnp.concatenate([base] * 4, axis=0)
        else:
            acc[:, at] += part

    tasks = []
    for k in range(2):
        stage = 2 * k
        for i, s in enumerate(sorted(shards, key=lambda s: (both[s + (k,)], s))):
            call = functools.partial(query_task, i == 0, *s, k)
            tasks.append((stage, -1, both[s + (k,)], QUERY_US, call))
        for shard in range(4 * k, 4 * k + 4):
            call = functools.partial(attend_task, shard)
            tasks.append((stage + 1, stage, 0, ATTEND_US, call))
    cut = 8 - LAST_SHARDS
    when = max(both[s + (2,)] for s in order)
    for start in range(0, 2048, 256):
        call = functools.partial(out_task, 0, 8, start, 256, 2)
        tasks.append((4, 3, when, OUT_US, call))
    for low, high, stage in ((0, cut, 5), (cut, 8, 6)):
        when = max(both[s + (3,)] for s in order[low:high])
        for start in range(2048, 4096, 512):
            call = functools.partial(out_task, low, high, start, 512, 3)
            tasks.append((stage, stage - 1, when, OUT_US * 2 * (high - low) / 8, call))

    def next_task(step, budget):
        for i, (stage, after, when, cost, call) in enumerate(tasks):
            if when <= step and cost <= budget and not any(t[0] <= after for t in tasks):
                if stage < 4 or i == 0:
                    tasks.pop(i)
                    return cost, call
        return None

    fetched = False
    for step in range(n_rounds + LAG):
        came = step - LAG
        if came >= 0:
            for link in range(3):
                for_places(
                    arrivals[came][link],
                    lambda options, weight, link=link: link_copy(
                        link, came, options, weight
                    ).wait_recv(),
                )
        if step < n_rounds:
            for link in range(3):
                for_places(
                    rounds[step][link],
                    lambda options, weight, link=link: link_copy(
                        link, step, options, weight
                    ).start(),
                )
        for group in mine:
            if mine[group] == step and step > 0:
                relay(*group)
        if step >= 1:
            if not fetched:
                fetches[2].wait()
                fetches[3].wait()
                fetched = True
            budget = ROUND_US
            while (found := next_task(step, budget)) is not None:
                budget -= found[0]
                found[1]()
    while tasks:
        next_task(1 << 20, 1 << 20)[1]()

    @pl.loop(0, 4)
    def _(member):
        latent = dp * 4 + member
        count = counts_ref[latent]
        total = jnp.int32(0)
        weights = [jnp.int32(0)] * 4
        for s in range(4):
            weight = jnp.where(s < count, guide_ref[s], 0)
            total = total + weight
            cond = conds_ref[s, latent]
            weights = [w + jnp.where(cond == c, weight, 0) for c, w in enumerate(weights)]
        share = 1.0 / jnp.full((32, 1), total.astype(jnp.float32))
        scale = 1.0 + scale_ref[pl.ds(member, 1), :]
        shift = shift_ref[pl.ds(member, 1), :]
        start = pl.multiple_of(member * 32, 32)
        rows = [pl.ds(pl.multiple_of(c * 128 + start, 32), 32) for c in range(4)]
        spans = [slice(j, j + 128) for j in range(0, 4096, 128)]
        centers, gains = [], []
        for c in range(4):
            summed = jnp.zeros((32, 128), jnp.float32)
            for at in spans:
                summed += acc[rows[c], at]
            centers.append(jnp.sum(summed, axis=-1, keepdims=True) / 4096)
        for c in range(4):
            summed = jnp.zeros((32, 128), jnp.float32)
            for at in spans:
                moved_h = acc[rows[c], at] - centers[c]
                summed += moved_h * moved_h
            spread = jnp.sum(summed, axis=-1, keepdims=True) / 4096
            gains.append(lax.rsqrt(spread + 1e-06) * (weights[c].astype(jnp.float32) * share))
        for at in spans:
            numer = jnp.zeros((32, 128), jnp.float32)
            for c in range(4):
                numer += (acc[rows[c], at] - centers[c]) * gains[c]
            combined = numer.astype(jnp.bfloat16).astype(jnp.float32)
            out_ref[pl.ds(start, 32), at] = (
                combined * scale[:, at] + shift[:, at]
            ).astype(jnp.bfloat16)

    for link in range(3):
        sends = [sum(row[link][p] is not None for row in rounds) for p in range(4)]
        for many in sorted(set(sends)):
            here = functools.reduce(
                jnp.logical_or, [place == p for p in range(4) if sends[p] == many]
            )
            pl.when(here)(
                functools.partial(wait_sent, send_sem.at[link], acc.at[pl.ds(0, many * 8)])
            )
    wait_sent(send_sem.at[3], wq.at[pl.ds(0, 7)])


def on_device(
    n_dp,
    latents,
    w_query,
    w_out,
    text_cache,
    branch_counts,
    branch_conds,
    guide_weights,
    mod_scale,
    mod_shift,
):
    members, rows_here, width = latents.shape
    rows = members * rows_here
    n_rounds = len(make_rounds()[0])
    anywhere = pl.BlockSpec(memory_space=pl.ANY)
    in_vmem = pl.BlockSpec(memory_space=pltpu.VMEM)
    in_smem = pl.BlockSpec(memory_space=pltpu.SMEM)
    mixed = pl.pallas_call(
        functools.partial(kernel, n_dp),
        out_shape=jax.ShapeDtypeStruct((rows, width), jnp.bfloat16),
        in_specs=[anywhere] * 4 + [in_smem] * 3 + [in_vmem] * 2,
        out_specs=in_vmem,
        scratch_shapes=[
            pltpu.VMEM((8, 512, 2048), jnp.bfloat16),
            pltpu.VMEM((8, 256, 4096), jnp.bfloat16),
            pltpu.VMEM((rows, width), jnp.bfloat16),
            pltpu.VMEM(text_cache.shape, jnp.bfloat16),
            pltpu.VMEM((rows, 2048), jnp.float32),
            pltpu.VMEM((4 * rows, 2048), jnp.bfloat16),
            pltpu.VMEM((4 * rows, width), jnp.float32),
            pltpu.SemaphoreType.DMA((4,)),
            pltpu.SemaphoreType.DMA((3 * n_rounds,)),
            pltpu.SemaphoreType.DMA((8 * KGROUPS,)),
            pltpu.SemaphoreType.DMA((4,)),
        ],
        compiler_params=pltpu.CompilerParams(
            collective_id=0, has_side_effects=True, vmem_limit_bytes=58 * 2**20
        ),
        name="gather_and_attend",
    )(
        latents.reshape(rows, width),
        w_query,
        w_out,
        text_cache,
        branch_counts,
        branch_conds.T,
        guide_weights,
        mod_scale,
        mod_shift,
    )
    return mixed.reshape(members, rows_here, width)


def solution(mesh):
    return jax.shard_map(
        functools.partial(on_device, mesh.shape["dp"]),
        mesh=mesh,
        in_specs=(
            P("dp", "fsdp", None),
            P("fsdp", None),
            P("fsdp", None),
            P(),
            P(),
            P(),
            P(),
            P("dp", None),
            P("dp", None),
        ),
        out_specs=P("dp", "fsdp", None),
        check_vma=False,
    )
```

time: 111 us -> 88.6 us (0.80)
  Pallas kernels: 108 us -> 86.2 us
    pallas_call x1, Pallas kernels: 108 us -> 86.2 us  [on_device(): pl.pallas_call(functools.partial(kernel, n_dp), out_shape=jax.ShapeDtypeS...]
where the time goes in v2:
time: 88.6 us; the launch traced here: 88.5 us
  Pallas kernels  86.2 us (97%)
  local copies, waits for them, and re-layouts  2.29 us (3%)
    pallas_call x1, Pallas kernels, on_device(): pl.pallas_call(functools.partial(kernel, n_dp), out_shape=jax.ShapeDtypeS...  86.2 us
    unnamed x1, local copies, waits for them, and re-layouts  2.29 us

profile of v2, /device:TPU:1, one launch (start us, length us, event | category | flops | bytes accessed | tf_op | source)
XLA Modules:
  0.0 88.5 jit_solution(3570391755936541706)
XLA Ops:
  0.0 86.2 %gather_and_attend.1 = bf16[128,4096]{1,0:T(8,128)(2,1)} custom-call(bf16[128,4096]{1,0:T(8,128)(2,1)} %bitcast.4, bf16[512,2048]{1,0:T(8,128)(2,1)} %wq_ref.1, bf16[256,4096]{1,0:T(8,128)(2,1)} %wo_ref.1, bf16[4,128,4096]{2,1,0:T(8,128)(2,1)} %text_ref.1, s32[128]{0:T(128)} %counts_ref.1, s32[4,128]{1,0:T(4,128)} %bitcast.5, s32[4]{0:T(128)} %guide_ref.1, ...), custom_call_target="tpu_custom_call" | custom-call | tf_op jit(solution)/shard_map/gather_and_attend/pallas_call | solution.py:458
  86.2 2.3 %copy.11 = bf16[4,32,4096]{2,1,0:T(8,128)(2,1)} copy(bf16[4,32,4096]{2,1,0:T(8,128)(2,1)} %bitcast.3) | data formatting | bytes 2097152

commit v3 on v2

--- a/solution.py
+++ b/solution.py
@@ -12,17 +12,54 @@
 MESH = pl.DeviceIdType.MESH
 LAG = 3
 KGROUPS = 4
-RELAY_LAG = 2
-PREFS = {
-    "x": (1.5859338734408208, 2.214087352289587, 2.9301547809913906),
-    "y": (1.1536104177094657, 1.5604518340377975, 1.8994994812664077),
-    "z": (-2.091808917993905, 1.831880295654794, -1.8133725211069505),
-}
-CHAIN_PREF = 2.3398409033170617
-GROUP_PREF = 0.5
-LINK_ORDER = (0, 2, 1)
-ROUND_US = 1.2
-QUERY_US, ATTEND_US, OUT_US = 0.27, 0.72, 0.72
+RELAY_LAG = (2, 2, 2, 1)
+ROUNDS = (
+    (-1, -1, -1, -1, 10, 8, 11, 9, -1, -1, -1, 3),
+    (-1, -1, -1, -1, 3, 0, 3, 11, -1, -1, -1, 2),
+    (-1, -1, -1, -1, 1, 4, 1, 7, -1, -1, -1, 11),
+    (19, 40, 43, 41, 42, 40, 43, 41, 19, -1, -1, 41),
+    (35, 32, 35, 43, 19, 6, 35, 14, 18, -1, 35, 43),
+    (33, 36, 33, 39, 6, 3, 6, 39, 42, 36, 33, 9),
+    (27, 72, 40, 73, 16, 11, 40, 6, 57, 19, 75, 42),
+    (59, 19, 67, 46, 5, 33, 67, 0, 51, 18, 67, 1),
+    (25, 38, 38, 71, 34, 38, 75, 40, 34, 42, 34, 39),
+    (74, 73, 72, 36, 11, 43, 19, 38, 58, 57, 19, 38),
+    (38, 65, 99, 67, 37, 65, 18, 47, 48, 65, 99, 67),
+    (55, 70, 107, 68, 18, 51, 39, 74, 17, 70, 107, 68),
+    (48, 58, 51, 19, 48, 73, 51, 34, 55, 58, 51, 37),
+    (39, 97, 96, 99, 39, 35, 73, 70, 69, 66, 65, 99),
+    (75, 83, 19, 79, 84, 83, 5, 71, 56, 17, 18, 69),
+    (80, 105, 71, 16, 80, 18, 58, 51, 53, 59, 48, 66),
+    (71, 98, 105, 96, 38, 69, 66, 66, 49, 55, 105, 102),
+    (116, 71, 73, 76, 33, 80, 37, 12, 116, 80, 58, 103),
+    (112, 106, 90, 48, 82, 53, 17, 83, 82, 115, 50, 83),
+    (72, 99, 55, 83, 118, 49, 55, 79, 118, 53, 55, 15),
+    (85, 116, 80, 77, 119, 68, 80, 58, 119, 116, 104, 44),
+    (67, 67, 91, 115, 117, 116, 91, 49, 114, 82, 57, 115),
+    (43, 107, 87, 55, 73, 81, 87, 50, 22, 118, 53, 73),
+    (60, 101, 116, 103, 31, 117, 81, 55, 23, 100, 116, 104),
+    (99, 53, 88, 112, 74, 20, 123, 90, 60, 20, 88, 107),
+    (40, 85, 53, 53, 89, 55, 82, 82, 26, 22, 119, 78),
+    (23, 102, 100, 116, 75, 58, 119, 116, 63, 21, 118, 116),
+    (96, 60, 59, 100, 15, 52, 89, 88, 24, 60, 27, 106),
+    (94, 26, 27, 88, 94, 15, 53, 119, 121, 86, 22, 114),
+    (107, 90, 123, 20, 58, 14, 15, 122, 94, 63, 59, 119),
+    (86, 24, 60, 120, 47, 63, 121, 52, 122, 26, 56, 118),
+    (126, 61, 101, 27, 126, 47, 60, 54, 126, 103, 85, 117),
+    (95, 91, 47, 122, 13, 46, 47, 59, 120, 94, 60, 46),
+    (79, 122, 61, 111, 56, 95, 13, 121, 89, 122, 61, 75),
+    (127, 95, 92, 44, 14, 79, 92, 78, 31, 126, 92, 13),
+    (92, 79, 94, -1, 45, 12, 79, 77, 30, 78, 63, 12),
+    (47, 127, 45, 61, 79, 61, 45, 61, 45, 127, 94, -1),
+    (124, 111, 124, -1, 76, 78, 126, 92, 29, 31, 126, -1),
+    (77, 76, 111, -1, 77, -1, 78, -1, 28, 76, 95, -1),
+    (-1, 124, -1, -1, -1, -1, 77, 93, -1, -1, 127, -1),
+    (-1, 108, 31, -1, -1, -1, -1, 124, -1, 29, 30, 126),
+    (-1, -1, -1, -1, -1, -1, -1, -1, -1, -1, 31, -1),
+    (-1, -1, -1, -1, -1, -1, -1, 125, -1, -1, -1, -1),
+)
+ROUND_US = 1.5
+QUERY_US, ATTEND_US, OUT_US, STATS_US = 0.27, 0.72, 0.72, 0.3
 LAST_SHARDS = 3
 
 
@@ -37,46 +74,22 @@
     return 0, (dy, 1 - h, k, r)
 
 
+def named(number):
+    return None if number < 0 else (number // 32, number // 16 % 2, number // 4 % 4, number % 4)
+
+
 def make_rounds():
-    pieces = [
-        (dy, h, k, r) for dy in range(4) for h in range(2) for k in range(KGROUPS) for r in range(4)
-    ]
-    ready = [{p: 0 if p[:2] == (0, 0) else 1 << 30 for p in pieces} for _ in range(4)]
-    taken = [{p: p[:2] == (0, 0) for p in pieces} for _ in range(4)]
-    worth = {}
-    for link, name in enumerate("xyz"):
-        half, depth, column = PREFS[name]
-        for p in pieces:
-            worth[link, p] = (
-                -GROUP_PREF * p[2]
-                + half * p[1]
-                + depth * p[0]
-                + column * p[3]
-            )
-    left = 4 * (len(pieces) - KGROUPS * 4)
-    rounds = []
-    while left:
-        now = len(rounds)
-        row = [[None] * 4 for _ in range(3)]
-        for link in LINK_ORDER:
+    rounds = [[[named(row[link * 4 + p]) for p in range(4)] for link in range(3)] for row in ROUNDS]
+    ready = [{named(n): 0 for n in range(16)} for _ in range(4)]
+    for now, row in enumerate(rounds):
+        for link in range(3):
             for place in range(4):
-                best, best_worth = None, -1e18
-                for p in pieces:
-                    if ready[place][p] <= now:
-                        to, there = moved(link, place, p)
-                        if not taken[to][there]:
-                            w = worth[link, there]
-                            if link == 2:
-                                w += CHAIN_PREF * there[1] * (3 - to)
-                            if w > best_worth:
-                                best, best_worth = (p, to, there), w
-                if best is not None:
-                    p, to, there = best
-                    taken[to][there] = True
+                piece = row[link][place]
+                if piece is not None:
+                    to, there = moved(link, place, piece)
+                    assert ready[place][piece] <= now and there not in ready[to]
                     ready[to][there] = now + LAG
-                    left -= 1
-                    row[link][place] = p
-        rounds.append(row)
+    assert all(len(r) == 128 for r in ready)
     return rounds, ready
 
 
@@ -100,7 +113,7 @@
             for k in range(KGROUPS):
                 mine[dy, h, k] = max(ready[place][dy, h, k, r] for place in range(4) for r in range(4))
     for dy, h, k in mine:
-        both[dy, h, k] = max(mine[dy, h, k], mine[(4 - dy) % 4, h, k] + RELAY_LAG)
+        both[dy, h, k] = max(mine[dy, h, k], mine[(4 - dy) % 4, h, k] + RELAY_LAG[k])
         if (dy, h) == (0, 0):
             both[dy, h, k] = 0
     return mine, both
@@ -125,6 +138,8 @@
     q_acc,
     att,
     acc,
+    half_center,
+    half_spread,
     send_sem,
     recv_sem,
     sib_sem,
@@ -159,14 +174,14 @@
         pltpu.make_async_copy(lat_ref, x_buf, local_sem.at[2]),
         pltpu.make_async_copy(text_ref, text, local_sem.at[3]),
     ]
-    for fetch in fetches:
+    for fetch in fetches[:3]:
         fetch.start()
     barrier = pltpu.get_barrier_semaphore()
     for other in sources + (sibling,):
         pl.semaphore_signal(barrier, inc=1, device_id=other, device_id_type=MESH)
     pl.semaphore_wait(barrier, 4)
     fetches[0].wait()
-    fetches[1].wait()
+    out_fetched = False
 
     shards = {
         (dy, h): ((y_at + 4 - sign * dy) % 4) * 2 + (z_hi + h) % 2 for dy in range(4) for h in range(2)
@@ -236,6 +251,18 @@
             return wq.at[shard, rows, pl.ds(k * 1024, 1024)], sib_sem.at[k * 8 + shard]
         rows = pl.ds(pl.multiple_of(of_core * 128, 128), 128)
         return wo.at[shard, rows, pl.ds((k - 2) * 2048, 2048)], sib_sem.at[k * 8 + shard]
+
+    def relay_piece(options, weight):
+        ref = slot(options, weight)
+        shard = pick(options, lambda p: (p[:2], shards[p[:2]]))
+        pltpu.make_async_remote_copy(
+            src_ref=ref,
+            dst_ref=ref,
+            send_sem=send_sem.at[3],
+            recv_sem=sib_sem.at[3 * 8 + shard],
+            device_id=sibling,
+            device_id_type=MESH,
+        ).start()
 
     def relay(dy, h, k):
         ref, sem = half_group(dy, h, k, core)
@@ -324,6 +351,20 @@
         else:
             acc[:, at] += part
 
+    def stats_task(start):
+        for low in range(start, start + 64, 32):
+            rows = slice(low, low + 32)
+            summed = jnp.zeros((32, 128), jnp.float32)
+            for j in range(0, 2048, 128):
+                summed += acc[rows, j : j + 128]
+            center = jnp.sum(summed, axis=-1, keepdims=True) / 2048
+            summed = jnp.zeros((32, 128), jnp.float32)
+            for j in range(0, 2048, 128):
+                moved_h = acc[rows, j : j + 128] - center
+                summed += moved_h * moved_h
+            half_center[rows] = jnp.broadcast_to(center, (32, 128))
+            half_spread[rows] = summed
+
     tasks = []
     for k in range(2):
         stage = 2 * k
@@ -338,18 +379,20 @@
     for start in range(0, 2048, 256):
         call = functools.partial(out_task, 0, 8, start, 256, 2)
         tasks.append((4, 3, when, OUT_US, call))
-    for low, high, stage in ((0, cut, 5), (cut, 8, 6)):
+    for start in range(0, 512, 64):
+        tasks.append((5, 4, 0, STATS_US, functools.partial(stats_task, start)))
+    for low, high, stage in ((0, cut, 6), (cut, 8, 7)):
         when = max(both[s + (3,)] for s in order[low:high])
         for start in range(2048, 4096, 512):
             call = functools.partial(out_task, low, high, start, 512, 3)
-            tasks.append((stage, stage - 1, when, OUT_US * 2 * (high - low) / 8, call))
+            after = 4 if stage == 6 else 6
+            tasks.append((stage, after, when, OUT_US * 2 * (high - low) / 8, call))
 
     def next_task(step, budget):
         for i, (stage, after, when, cost, call) in enumerate(tasks):
             if when <= step and cost <= budget and not any(t[0] <= after for t in tasks):
-                if stage < 4 or i == 0:
-                    tasks.pop(i)
-                    return cost, call
+                tasks.pop(i)
+                return cost, call
         return None
 
     fetched = False
@@ -364,6 +407,9 @@
                     ).wait_recv(),
                 )
         if step < n_rounds:
+            if not out_fetched and any(p is not None and p[2] > 1 for got in rounds[step] for p in got):
+                fetches[1].wait()
+                out_fetched = True
             for link in range(3):
                 for_places(
                     rounds[step][link],
@@ -371,8 +417,14 @@
                         link, step, options, weight
                     ).start(),
                 )
+            if step == 0:
+                fetches[3].start()
+        if came >= 0:
+            for link in range(3):
+                last_group = [p if p is not None and p[2] == 3 else None for p in arrivals[came][link]]
+                for_places(last_group, relay_piece)
         for group in mine:
-            if mine[group] == step and step > 0:
+            if mine[group] == step and step > 0 and group[2] < 3:
                 relay(*group)
         if step >= 1:
             if not fetched:
@@ -403,23 +455,24 @@
         start = pl.multiple_of(member * 32, 32)
         rows = [pl.ds(pl.multiple_of(c * 128 + start, 32), 32) for c in range(4)]
         spans = [slice(j, j + 128) for j in range(0, 4096, 128)]
-        centers, gains = [], []
+        gains, offset = [], jnp.zeros((32, 1), jnp.float32)
         for c in range(4):
-            summed = jnp.zeros((32, 128), jnp.float32)
-            for at in spans:
-                summed += acc[rows[c], at]
-            centers.append(jnp.sum(summed, axis=-1, keepdims=True) / 4096)
-        for c in range(4):
-            summed = jnp.zeros((32, 128), jnp.float32)
-            for at in spans:
-                moved_h = acc[rows[c], at] - centers[c]
-                summed += moved_h * moved_h
-            spread = jnp.sum(summed, axis=-1, keepdims=True) / 4096
-            gains.append(lax.rsqrt(spread + 1e-06) * (weights[c].astype(jnp.float32) * share))
+            pivot = half_center[rows[c]]
+            summed, squares = jnp.zeros((32, 128), jnp.float32), half_spread[rows[c]]
+            for at in spans[16:]:
+                moved_h = acc[rows[c], at] - pivot
+                summed += moved_h
+                squares += moved_h * moved_h
+            shift_c = jnp.sum(summed, axis=-1, keepdims=True) / 4096
+            spread = jnp.sum(squares, axis=-1, keepdims=True) / 4096 - shift_c * shift_c
+            spread = jnp.maximum(spread, 0.0)
+            gain = lax.rsqrt(spread + 1e-06) * (weights[c].astype(jnp.float32) * share)
+            gains.append(gain)
+            offset += (pivot[:, :1] + shift_c) * gain
         for at in spans:
-            numer = jnp.zeros((32, 128), jnp.float32)
+            numer = -offset
             for c in range(4):
-                numer += (acc[rows[c], at] - centers[c]) * gains[c]
+                numer += acc[rows[c], at] * gains[c]
             combined = numer.astype(jnp.bfloat16).astype(jnp.float32)
             out_ref[pl.ds(start, 32), at] = (
                 combined * scale[:, at] + shift[:, at]
@@ -468,6 +521,8 @@
             pltpu.VMEM((rows, 2048), jnp.float32),
             pltpu.VMEM((4 * rows, 2048), jnp.bfloat16),
             pltpu.VMEM((4 * rows, width), jnp.float32),
+            pltpu.VMEM((4 * rows, 128), jnp.float32),
+            pltpu.VMEM((4 * rows, 128), jnp.float32),
             pltpu.SemaphoreType.DMA((4,)),
             pltpu.SemaphoreType.DMA((3 * n_rounds,)),
             pltpu.SemaphoreType.DMA((8 * KGROUPS,)),

time: 88.6 us -> 85.4 us (0.964)
  Pallas kernels: 86.2 us -> 82.9 us
    pallas_call x1, Pallas kernels: 86.2 us -> 82.9 us  [on_device(): pl.pallas_call(functools.partial(kernel, n_dp), out_shape=jax.ShapeDtypeS...]
where the time goes in v3:
time: 85.4 us; the launch traced here: 85.2 us
  Pallas kernels  82.9 us (97%)
  local copies, waits for them, and re-layouts  2.29 us (3%)
    pallas_call x1, Pallas kernels, on_device(): pl.pallas_call(functools.partial(kernel, n_dp), out_shape=jax.ShapeDtypeS...  82.9 us
    unnamed x1, local copies, waits for them, and re-layouts  2.29 us

profile of v3, /device:TPU:1, one launch (start us, length us, event | category | flops | bytes accessed | tf_op | source)
XLA Modules:
  0.0 85.2 jit_solution(17037932252759063861)
XLA Ops:
  0.0 82.9 %gather_and_attend.1 = bf16[128,4096]{1,0:T(8,128)(2,1)} custom-call(bf16[128,4096]{1,0:T(8,128)(2,1)} %bitcast.4, bf16[512,2048]{1,0:T(8,128)(2,1)} %wq_ref.1, bf16[256,4096]{1,0:T(8,128)(2,1)} %wo_ref.1, bf16[4,128,4096]{2,1,0:T(8,128)(2,1)} %text_ref.1, s32[128]{0:T(128)} %counts_ref.1, s32[4,128]{1,0:T(4,128)} %bitcast.5, s32[4]{0:T(128)} %guide_ref.1, ...), custom_call_target="tpu_custom_call" | custom-call | tf_op jit(solution)/shard_map/gather_and_attend/pallas_call | solution.py:511
  82.9 2.3 %copy.11 = bf16[4,32,4096]{2,1,0:T(8,128)(2,1)} copy(bf16[4,32,4096]{2,1,0:T(8,128)(2,1)} %bitcast.3) | data formatting | bytes 2097152

commit v4 on v3

--- a/solution.py
+++ b/solution.py
@@ -58,8 +58,8 @@
     (-1, -1, -1, -1, -1, -1, -1, -1, -1, -1, 31, -1),
     (-1, -1, -1, -1, -1, -1, -1, 125, -1, -1, -1, -1),
 )
-ROUND_US = 1.5
-QUERY_US, ATTEND_US, OUT_US, STATS_US = 0.27, 0.72, 0.72, 0.3
+ROUND_US = 1.9
+QUERY_US, ATTEND_US, OUT_US = 0.27, 0.72, 0.72
 LAST_SHARDS = 3
 
 
@@ -138,8 +138,10 @@
     q_acc,
     att,
     acc,
-    half_center,
-    half_spread,
+    pivot,
+    distance,
+    square,
+    out_buf,
     send_sem,
     recv_sem,
     sib_sem,
@@ -335,6 +337,22 @@
             at = pl.ds(pl.multiple_of(places_of[shard] + p * HDIM, HDIM), HDIM)
             att[pl.ds(cond * 128, 128), at] = result.astype(jnp.bfloat16)
 
+    def tally(rows, value, width, first):
+        if first:
+            center = jnp.sum(value, axis=-1, keepdims=True) / width
+            from_here = jnp.broadcast_to(center, (128, 128))
+            pivot[rows] = from_here
+            summed = jnp.zeros((128, 128), jnp.float32)
+            squared = jnp.zeros((128, 128), jnp.float32)
+        else:
+            from_here, summed, squared = pivot[rows], distance[rows], square[rows]
+        for j in range(0, width, 128):
+            moved_h = value[:, j : j + 128] - from_here
+            summed += moved_h
+            squared += moved_h * moved_h
+        distance[rows] = summed
+        square[rows] = squared
+
     def out_task(low, high, start, width, k):
         if start == (k - 2) * 2048:
             for dy, h in order[low:high]:
@@ -345,25 +363,16 @@
             jnp.concatenate([wo[shards[s], :, at] for s in order[low:high]], axis=0),
             preferred_element_type=jnp.float32,
         )
-        if low == 0:
-            base = x_buf[:, at].astype(jnp.float32)
-            acc[:, at] = part + jnp.concatenate([base] * 4, axis=0)
-        else:
-            acc[:, at] += part
-
-    def stats_task(start):
-        for low in range(start, start + 64, 32):
-            rows = slice(low, low + 32)
-            summed = jnp.zeros((32, 128), jnp.float32)
-            for j in range(0, 2048, 128):
-                summed += acc[rows, j : j + 128]
-            center = jnp.sum(summed, axis=-1, keepdims=True) / 2048
-            summed = jnp.zeros((32, 128), jnp.float32)
-            for j in range(0, 2048, 128):
-                moved_h = acc[rows, j : j + 128] - center
-                summed += moved_h * moved_h
-            half_center[rows] = jnp.broadcast_to(center, (32, 128))
-            half_spread[rows] = summed
+        base = x_buf[:, at].astype(jnp.float32)
+        for c in range(4):
+            rows = slice(c * 128, c * 128 + 128)
+            if low == 0:
+                value = part[rows] + base
+            else:
+                value = part[rows] + acc[rows, at]
+            acc[rows, at] = value
+            if k == 2 or low > 0:
+                tally(rows, value, width, k == 2 and start == 0)
 
     tasks = []
     for k in range(2):
@@ -379,8 +388,6 @@
     for start in range(0, 2048, 256):
         call = functools.partial(out_task, 0, 8, start, 256, 2)
         tasks.append((4, 3, when, OUT_US, call))
-    for start in range(0, 512, 64):
-        tasks.append((5, 4, 0, STATS_US, functools.partial(stats_task, start)))
     for low, high, stage in ((0, cut, 6), (cut, 8, 7)):
         when = max(both[s + (3,)] for s in order[low:high])
         for start in range(2048, 4096, 512):
@@ -457,26 +464,22 @@
         spans = [slice(j, j + 128) for j in range(0, 4096, 128)]
         gains, offset = [], jnp.zeros((32, 1), jnp.float32)
         for c in range(4):
-            pivot = half_center[rows[c]]
-            summed, squares = jnp.zeros((32, 128), jnp.float32), half_spread[rows[c]]
-            for at in spans[16:]:
-                moved_h = acc[rows[c], at] - pivot
-                summed += moved_h
-                squares += moved_h * moved_h
-            shift_c = jnp.sum(summed, axis=-1, keepdims=True) / 4096
-            spread = jnp.sum(squares, axis=-1, keepdims=True) / 4096 - shift_c * shift_c
+            shift_c = jnp.sum(distance[rows[c]], axis=-1, keepdims=True) / 4096
+            spread = jnp.sum(square[rows[c]], axis=-1, keepdims=True) / 4096 - shift_c * shift_c
             spread = jnp.maximum(spread, 0.0)
             gain = lax.rsqrt(spread + 1e-06) * (weights[c].astype(jnp.float32) * share)
             gains.append(gain)
-            offset += (pivot[:, :1] + shift_c) * gain
+            offset += (pivot[rows[c], :1] + shift_c) * gain
         for at in spans:
             numer = -offset
             for c in range(4):
                 numer += acc[rows[c], at] * gains[c]
             combined = numer.astype(jnp.bfloat16).astype(jnp.float32)
-            out_ref[pl.ds(start, 32), at] = (
+            out_buf[pl.ds(start, 32), at] = (
                 combined * scale[:, at] + shift[:, at]
             ).astype(jnp.bfloat16)
+        done = pl.ds(start, 32)
+        pltpu.make_async_copy(out_buf.at[done], out_ref.at[done], local_sem.at[4]).start()
 
     for link in range(3):
         sends = [sum(row[link][p] is not None for row in rounds) for p in range(4)]
@@ -488,6 +491,7 @@
                 functools.partial(wait_sent, send_sem.at[link], acc.at[pl.ds(0, many * 8)])
             )
     wait_sent(send_sem.at[3], wq.at[pl.ds(0, 7)])
+    pltpu.make_async_copy(out_buf, out_ref, local_sem.at[4]).wait()
 
 
 def on_device(
@@ -512,7 +516,7 @@
         functools.partial(kernel, n_dp),
         out_shape=jax.ShapeDtypeStruct((rows, width), jnp.bfloat16),
         in_specs=[anywhere] * 4 + [in_smem] * 3 + [in_vmem] * 2,
-        out_specs=in_vmem,
+        out_specs=anywhere,
         scratch_shapes=[
             pltpu.VMEM((8, 512, 2048), jnp.bfloat16),
             pltpu.VMEM((8, 256, 4096), jnp.bfloat16),
@@ -523,10 +527,12 @@
             pltpu.VMEM((4 * rows, width), jnp.float32),
             pltpu.VMEM((4 * rows, 128), jnp.float32),
             pltpu.VMEM((4 * rows, 128), jnp.float32),
+            pltpu.VMEM((4 * rows, 128), jnp.float32),
+            pltpu.VMEM((rows, width), jnp.bfloat16),
             pltpu.SemaphoreType.DMA((4,)),
             pltpu.SemaphoreType.DMA((3 * n_rounds,)),
             pltpu.SemaphoreType.DMA((8 * KGROUPS,)),
-            pltpu.SemaphoreType.DMA((4,)),
+            pltpu.SemaphoreType.DMA((5,)),
         ],
         compiler_params=pltpu.CompilerParams(
             collective_id=0, has_side_effects=True, vmem_limit_bytes=58 * 2**20

time: 85.4 us -> 84.6 us (level)
  no operation moved by 1% of the time
where the time goes in v4:
time: 84.6 us; the launch traced here: 84.5 us
  Pallas kernels  82.2 us (97%)
  local copies, waits for them, and re-layouts  2.29 us (3%)
    pallas_call x1, Pallas kernels, on_device(): pl.pallas_call(functools.partial(kernel, n_dp), out_shape=jax.ShapeDtypeS...  82.2 us
    unnamed x1, local copies, waits for them, and re-layouts  2.29 us

profile of v4, /device:TPU:1, one launch (start us, length us, event | category | flops | bytes accessed | tf_op | source)
XLA Modules:
  0.0 84.5 jit_solution(5047518613998058994)
XLA Ops:
  0.0 82.2 %gather_and_attend.1 = bf16[128,4096]{1,0:T(8,128)(2,1)} custom-call(bf16[128,4096]{1,0:T(8,128)(2,1)} %bitcast.4, bf16[512,2048]{1,0:T(8,128)(2,1)} %wq_ref.1, bf16[256,4096]{1,0:T(8,128)(2,1)} %wo_ref.1, bf16[4,128,4096]{2,1,0:T(8,128)(2,1)} %text_ref.1, s32[128]{0:T(128)} %counts_ref.1, s32[4,128]{1,0:T(4,128)} %bitcast.5, s32[4]{0:T(128)} %guide_ref.1, ...), custom_call_target="tpu_custom_call" | custom-call | tf_op jit(solution)/shard_map/gather_and_attend/pallas_call | solution.py:515
  82.2 2.3 %copy.11 = bf16[4,32,4096]{2,1,0:T(8,128)(2,1)} copy(bf16[4,32,4096]{2,1,0:T(8,128)(2,1)} %bitcast.3) | data formatting | bytes 2097152

commit v5 on v4

--- a/solution.py
+++ b/solution.py
@@ -14,49 +14,49 @@
 KGROUPS = 4
 RELAY_LAG = (2, 2, 2, 1)
 ROUNDS = (
-    (-1, -1, -1, -1, 10, 8, 11, 9, -1, -1, -1, 3),
-    (-1, -1, -1, -1, 3, 0, 3, 11, -1, -1, -1, 2),
-    (-1, -1, -1, -1, 1, 4, 1, 7, -1, -1, -1, 11),
-    (19, 40, 43, 41, 42, 40, 43, 41, 19, -1, -1, 41),
-    (35, 32, 35, 43, 19, 6, 35, 14, 18, -1, 35, 43),
-    (33, 36, 33, 39, 6, 3, 6, 39, 42, 36, 33, 9),
-    (27, 72, 40, 73, 16, 11, 40, 6, 57, 19, 75, 42),
-    (59, 19, 67, 46, 5, 33, 67, 0, 51, 18, 67, 1),
-    (25, 38, 38, 71, 34, 38, 75, 40, 34, 42, 34, 39),
-    (74, 73, 72, 36, 11, 43, 19, 38, 58, 57, 19, 38),
-    (38, 65, 99, 67, 37, 65, 18, 47, 48, 65, 99, 67),
-    (55, 70, 107, 68, 18, 51, 39, 74, 17, 70, 107, 68),
-    (48, 58, 51, 19, 48, 73, 51, 34, 55, 58, 51, 37),
-    (39, 97, 96, 99, 39, 35, 73, 70, 69, 66, 65, 99),
-    (75, 83, 19, 79, 84, 83, 5, 71, 56, 17, 18, 69),
-    (80, 105, 71, 16, 80, 18, 58, 51, 53, 59, 48, 66),
-    (71, 98, 105, 96, 38, 69, 66, 66, 49, 55, 105, 102),
-    (116, 71, 73, 76, 33, 80, 37, 12, 116, 80, 58, 103),
-    (112, 106, 90, 48, 82, 53, 17, 83, 82, 115, 50, 83),
-    (72, 99, 55, 83, 118, 49, 55, 79, 118, 53, 55, 15),
-    (85, 116, 80, 77, 119, 68, 80, 58, 119, 116, 104, 44),
-    (67, 67, 91, 115, 117, 116, 91, 49, 114, 82, 57, 115),
-    (43, 107, 87, 55, 73, 81, 87, 50, 22, 118, 53, 73),
-    (60, 101, 116, 103, 31, 117, 81, 55, 23, 100, 116, 104),
-    (99, 53, 88, 112, 74, 20, 123, 90, 60, 20, 88, 107),
-    (40, 85, 53, 53, 89, 55, 82, 82, 26, 22, 119, 78),
-    (23, 102, 100, 116, 75, 58, 119, 116, 63, 21, 118, 116),
-    (96, 60, 59, 100, 15, 52, 89, 88, 24, 60, 27, 106),
-    (94, 26, 27, 88, 94, 15, 53, 119, 121, 86, 22, 114),
-    (107, 90, 123, 20, 58, 14, 15, 122, 94, 63, 59, 119),
-    (86, 24, 60, 120, 47, 63, 121, 52, 122, 26, 56, 118),
-    (126, 61, 101, 27, 126, 47, 60, 54, 126, 103, 85, 117),
-    (95, 91, 47, 122, 13, 46, 47, 59, 120, 94, 60, 46),
-    (79, 122, 61, 111, 56, 95, 13, 121, 89, 122, 61, 75),
-    (127, 95, 92, 44, 14, 79, 92, 78, 31, 126, 92, 13),
-    (92, 79, 94, -1, 45, 12, 79, 77, 30, 78, 63, 12),
-    (47, 127, 45, 61, 79, 61, 45, 61, 45, 127, 94, -1),
-    (124, 111, 124, -1, 76, 78, 126, 92, 29, 31, 126, -1),
-    (77, 76, 111, -1, 77, -1, 78, -1, 28, 76, 95, -1),
-    (-1, 124, -1, -1, -1, -1, 77, 93, -1, -1, 127, -1),
-    (-1, 108, 31, -1, -1, -1, -1, 124, -1, 29, 30, 126),
-    (-1, -1, -1, -1, -1, -1, -1, -1, -1, -1, 31, -1),
-    (-1, -1, -1, -1, -1, -1, -1, 125, -1, -1, -1, -1),
+    (-1, -1, -1, -1, 4, 4, 3, 7, -1, -1, -1, 5),
+    (-1, -1, -1, -1, 6, 5, 2, 3, -1, -1, -1, 7),
+    (-1, -1, -1, -1, 7, 6, 7, 6, -1, -1, -1, 0),
+    (21, -1, 35, 39, 36, 7, 35, 39, 21, 36, -1, 39),
+    (23, -1, -1, 35, 38, 37, 8, 35, 23, 37, 34, 9),
+    (16, -1, -1, -1, 39, 38, 39, 38, 16, 38, -1, 3),
+    (68, 21, 67, 36, 3, 21, 67, 36, 68, 21, -1, 36),
+    (36, 23, 40, 32, 21, 39, 37, 67, 25, 23, 40, 67),
+    (17, 16, 71, 67, 71, 70, 71, 34, 19, 70, -1, 34),
+    (35, 53, 21, 68, 25, 68, 64, 68, 52, 16, 21, 32),
+    (53, 25, 23, 40, 53, 71, 69, 40, 83, 53, 23, 99),
+    (103, 17, 103, 64, 19, 53, 23, 66, 50, 102, 103, 66),
+    (32, 100, 16, 21, 69, 54, 41, 69, 48, 54, 96, 12),
+    (85, 54, 96, 23, 85, 1, 53, 72, 115, 83, 53, 72),
+    (115, 50, 55, 72, 82, 3, 55, 65, 82, 26, 16, 103),
+    (101, 48, 17, 101, 9, 48, 17, 22, 28, 50, 17, 65),
+    (28, 115, 83, 104, 88, 55, 83, 53, 117, 33, 83, 64),
+    (112, 33, 73, 73, 8, 35, 26, 16, 114, 82, 26, 73),
+    (117, 28, 18, 17, 41, 86, 49, 54, 81, 51, 49, 40),
+    (86, 112, 85, 83, 120, 87, 52, 83, 32, 117, 50, 33),
+    (119, 67, 115, 26, 52, 67, 58, 23, 120, 28, 82, 74),
+    (29, 29, 97, 18, 2, 26, 81, 74, 56, 48, 81, 105),
+    (73, 87, 117, 115, 14, 34, 82, 11, 24, 29, 51, 115),
+    (90, 99, 90, 27, 33, 33, 74, 82, 116, 120, 28, 80),
+    (30, 30, 58, 55, 34, 58, 33, 81, 121, 56, 90, 106),
+    (99, 56, 29, 86, 46, 56, 73, 43, 73, 24, 117, 43),
+    (74, 96, 120, 28, 65, 66, 84, 27, 89, 66, 120, 114),
+    (66, 90, 56, 106, 74, 90, 56, 52, 40, 31, 58, 11),
+    (122, 73, 24, 117, 40, 12, 91, 90, 59, 119, 91, 10),
+    (57, 26, 121, 120, 75, 10, 10, 87, 78, 89, 116, 59),
+    (78, 40, 106, 41, 29, 40, 31, 24, 106, -1, 88, 58),
+    (46, 122, 74, 122, 28, 73, 123, 15, 75, 44, 25, 120),
+    (-1, 78, 42, 29, 12, 78, 14, 13, 43, 78, 89, 121),
+    (79, 106, 107, 56, 61, 72, 63, 29, 61, 72, 31, -1),
+    (61, 44, 44, 47, 60, 14, 44, 47, 47, -1, 63, 47),
+    (44, 110, 46, 45, 79, 44, 30, 45, 60, 110, 78, -1),
+    (93, 61, 95, 61, 93, 31, 95, 61, 93, 79, 95, -1),
+    (76, -1, 76, 79, 92, 45, 76, 79, 92, 61, -1, 79),
+    (111, 111, 110, 63, 78, -1, 62, 77, -1, 60, 110, -1),
+    (125, 93, 92, 95, -1, 63, 92, 62, 125, -1, 127, -1),
+    (-1, -1, 108, 111, 77, 77, -1, 93, 124, -1, -1, 111),
+    (-1, -1, -1, -1, -1, -1, 94, -1, -1, -1, -1, -1),
+    (-1, 125, 124, 127, -1, 95, -1, 94, -1, -1, -1, -1),
 )
 ROUND_US = 1.9
 QUERY_US, ATTEND_US, OUT_US = 0.27, 0.72, 0.72

time: 84.6 us -> 84 us (level)
  no operation moved by 1% of the time
where the time goes in v5:
time: 84 us; the launch traced here: 83.8 us
  Pallas kernels  81.5 us (97%)
  local copies, waits for them, and re-layouts  2.29 us (3%)
    pallas_call x1, Pallas kernels, on_device(): pl.pallas_call(functools.partial(kernel, n_dp), out_shape=jax.ShapeDtypeS...  81.5 us
    unnamed x1, local copies, waits for them, and re-layouts  2.29 us

profile of v5, /device:TPU:1, one launch (start us, length us, event | category | flops | bytes accessed | tf_op | source)
XLA Modules:
  0.0 83.8 jit_solution(10822066635740887667)
XLA Ops:
  0.0 81.5 %gather_and_attend.1 = bf16[128,4096]{1,0:T(8,128)(2,1)} custom-call(bf16[128,4096]{1,0:T(8,128)(2,1)} %bitcast.4, bf16[512,2048]{1,0:T(8,128)(2,1)} %wq_ref.1, bf16[256,4096]{1,0:T(8,128)(2,1)} %wo_ref.1, bf16[4,128,4096]{2,1,0:T(8,128)(2,1)} %text_ref.1, s32[128]{0:T(128)} %counts_ref.1, s32[4,128]{1,0:T(4,128)} %bitcast.5, s32[4]{0:T(128)} %guide_ref.1, ...), custom_call_target="tpu_custom_call" | custom-call | tf_op jit(solution)/shard_map/gather_and_attend/pallas_call | solution.py:515
  81.5 2.3 %copy.11 = bf16[4,32,4096]{2,1,0:T(8,128)(2,1)} copy(bf16[4,32,4096]{2,1,0:T(8,128)(2,1)} %bitcast.3) | data formatting | bytes 2097152
